TPU v7x, 256 devices: a whole 4x4x8 slice. The times are simulated.
256 devices in a mesh: group: 64 (over x, y, z_lo), seq: 4 (over z_hi, core).
Axes of the slice: x: 4, y: 4, z: 8 (z_hi: 2, z_lo: 4; z = z_hi * 4 + z_lo), core: 2. Of those that a mesh axis runs over, the one named last changes fastest.
Arguments:
- queries: bfloat16 [32768, 6144], P(('group', 'seq')), may hold values from -32 to 32
- keys: bfloat16 [32768, 6144], P(('group', 'seq')), may hold values from -32 to 32
- values: bfloat16 [32768, 6144], P(('group', 'seq')), may hold values from -6 to 6
- noise_level: int32 [64], replicated, may hold values from 0 to 7
- block_mask: int32 [64, 3], replicated, may hold values 0 or 1
- gate_table: float32 [8, 6144], replicated, may hold values from 0.5 to 2
Outputs:
- gated: bfloat16 [32768, 6144], P(('group', 'seq'))
All inputs are finite; a program needn't handle non-finite values.
Results may differ from a plain program's by a relative error of at most 0.008.
Values may be sent and summed in bfloat16 or wider, within the bound.
A program may use at most 128 MiB of HBM per device.

v0:
```python
import jax
import jax.numpy as jnp
from jax import lax
from jax.sharding import PartitionSpec as P

HD = 128
WINDOW = 3
LEVELS = 8


def shifted(x, axis, by):
    length = lax.axis_size(axis)
    pairs = [(i, i + by) for i in range(length) if 0 <= i + by < length]
    return lax.ppermute(x, axis, pairs)


def shards(queries, keys, values, noise_level, block_mask, gate_table):
    query_cols, key_cols, value_cols = (
        lax.all_to_all(queries, "seq", split_axis=1, concat_axis=0, tiled=True),
        lax.all_to_all(keys, "seq", split_axis=1, concat_axis=0, tiled=True),
        lax.all_to_all(values, "seq", split_axis=1, concat_axis=0, tiled=True),
    )
    group_tokens = query_cols.shape[0]
    heads_here = query_cols.shape[1] // HD
    group_index = lax.axis_index("group")
    local_pair = jnp.stack([key_cols, value_cols])
    blocks = [local_pair] + [
        shifted(local_pair, "group", offset) for offset in range(1, WINDOW + 1)
    ]
    mask_row = lax.dynamic_index_in_dim(block_mask, group_index, 0, keepdims=False)
    query_heads = query_cols.reshape(group_tokens, heads_here, HD)
    scale = HD ** (-0.5)
    running = None
    for offset in range(WINDOW + 1):
        key_heads = blocks[offset][0].reshape(group_tokens, heads_here, HD)
        value_heads = blocks[offset][1].reshape(group_tokens, heads_here, HD)
        scores = (
            jnp.einsum("qhd,khd->hqk", query_heads, key_heads, preferred_element_type=jnp.float32)
            * scale
        )
        if offset > 0:
            visible = (group_index - offset >= 0) & (mask_row[offset - 1] == 1)
            scores = jnp.where(visible, scores, jnp.float32(-1e30))
        block_max = jnp.max(scores, axis=-1)
        if running is None:
            new_max = block_max
        else:
            new_max = jnp.maximum(running, block_max)
        weights = jnp.exp(scores - new_max[:, :, None])
        block_total = jnp.sum(weights, axis=-1)
        contribution = jnp.einsum(
            "hqk,khd->qhd",
            weights.astype(jnp.bfloat16),
            value_heads,
            preferred_element_type=jnp.float32,
        )
        if running is None:
            total = block_total
            accumulated = contribution
        else:
            factor = jnp.exp(running - new_max)
            total = total * factor + block_total
            accumulated = accumulated * jnp.transpose(factor)[:, :, None] + contribution
        running = new_max
    attended = (
        (accumulated / jnp.transpose(total)[:, :, None])
        .reshape(group_tokens, heads_here * HD)
        .astype(jnp.bfloat16)
    )
    token_rows = lax.all_to_all(attended, "seq", split_axis=0, concat_axis=1, tiled=True)
    level_index = lax.dynamic_index_in_dim(noise_level, group_index, 0, keepdims=False)
    one_hot = (jnp.arange(LEVELS) == level_index).astype(jnp.float32)
    gate_row = jnp.sum(one_hot[:, None] * gate_table, axis=0)
    return (token_rows.astype(jnp.float32) * gate_row[None, :]).astype(jnp.bfloat16)


def solution(mesh):
    placed = (
        P(("group", "seq"), None),
        P(("group", "seq"), None),
        P(("group", "seq"), None),
        P(),
        P(),
        P(),
    )
    return jax.shard_map(
        shards, mesh=mesh, in_specs=placed, out_specs=P(("group", "seq"), None), check_vma=False
    )
```

profile of v0, /device:TPU:64, one launch (start us, length us, event | category | flops | bytes accessed | tf_op | source)
XLA Modules:
  0.0 508.4 jit_solution(4198814420488175338)
XLA Ops:
  2.7 6.7 %all-to-all-start.1 = ((bf16[128,4,1536]{0,2,1:T(8,128)(2,1)}), bf16[128,4,1536]{0,2,1:T(8,128)(2,1)S(1)}, u32[]{:S(2)}, u32[]{:S(2)}) async-start(bf16[128,4,1536]{0,2,1:T(8,128)(2,1)} %bitcast.2), calls=%async_computation.1 | async-start | bytes 3145728 | tf_op jit(solution)/shard_map/all_to_all | solution.py:20
  10.9 39.0 %all-to-all-done.1 = bf16[128,4,1536]{0,2,1:T(8,128)(2,1)S(1)} async-done(((bf16[128,4,1536]{0,2,1:T(8,128)(2,1)}), bf16[128,4,1536]{0,2,1:T(8,128)(2,1)S(1)}, u32[]{:S(2)}, u32[]{:S(2)}) %all-to-all-start.1) | async-done | bytes 1572896 | tf_op jit(solution)/shard_map/all_to_all | solution.py:20
  50.0 3.6 all-to-all-start.2
  56.2 38.2 %all-to-all-done.2 = bf16[128,4,1536]{0,2,1:T(8,128)(2,1)S(1)} async-done(((bf16[128,4,1536]{0,2,1:T(8,128)(2,1)}), bf16[128,4,1536]{0,2,1:T(8,128)(2,1)S(1)}, u32[]{:S(2)}, u32[]{:S(2)}) %all-to-all-start.2) | async-done | bytes 1572896 | tf_op jit(solution)/shard_map/all_to_all | solution.py:21
  94.4 4.4 all-to-all-start
  98.7 7.3 %copy.61 = bf16[4,128,1536]{1,0,2:T(4,128)(2,1)S(1)} copy(bf16[4,128,1536]{1,2,0:T(8,128)(2,1)S(1)} %bitcast.154) | data formatting | bytes 3145728 | tf_op jit(solution)/shard_map/all_to_all | solution.py:20
  108.1 7.6 %copy.65 = bf16[4,128,1536]{1,0,2:T(4,128)(2,1)S(1)} copy(bf16[4,128,1536]{1,2,0:T(8,128)(2,1)} %bitcast.155) | data formatting | bytes 3145728 | tf_op jit(solution)/shard_map/all_to_all | solution.py:21
  121.8 3.4 collective-permute-start.1
  125.3 3.9 collective-permute-start
  135.8 4.6 collective-permute-start.2
  140.5 8.5 %copy.59 = bf16[4,128,1536]{1,0,2:T(4,128)(2,1)} copy(bf16[4,128,1536]{1,2,0:T(8,128)(2,1)} %bitcast.1) | data formatting | bytes 3145728 | tf_op jit(solution)/shard_map/all_to_all | solution.py:19
  151.5 7.9 %multiply_reduce_fusion = (f32[12,512]{1,0:T(8,128)S(1)}, f32[12,512,512]{1,2,0:T(8,128)}) fusion(bf16[512,12,128]{0,2,1:T(8,128)(2,1)S(1)} %reshape.69, bf16[512,12,128]{0,2,1:T(8,128)(2,1)} %reshape_squeeze_stack.6), kind=kOutput, calls=%fused_computation.13 | convolution fusion | flops 811591680 | bytes 15753216 | tf_op jit(solution)/shard_map/qhd,khd->hqk/dot_general | solution.py:38
  159.4 9.0 %fusion.17 = f32[12,512,128]{2,1,0:T(8,128)} fusion(bf16[512,12,128]{0,2,1:T(8,128)(2,1)S(1)} %copy-done.2, f32[12,512,512]{1,2,0:T(8,128)} %get-tuple-element.26, f32[12,512]{1,0:T(8,128)S(1)} %get-tuple-element.25), kind=kOutput, calls=%fused_computation.25 | convolution fusion | flops 814743552 | bytes 17326080 | tf_op jit(solution)/shard_map/hqk,khd->qhd/dot_general | solution.py:51
  168.4 6.8 %fusion.3 = f32[12,512]{1,0:T(8,128)S(1)} fusion(f32[12,512,512]{1,2,0:T(8,128)} %get-tuple-element.26, f32[12,512]{1,0:T(8,128)S(1)} %get-tuple-element.25), kind=kLoop, calls=%fused_computation.14 | loop fusion | flops 9431040 | bytes 12632064 | tf_op jit(solution)/shard_map/reduce_sum | solution.py:50
  175.2 165.1 %collective-permute-done.1 = bf16[2,512,1536]{1,2,0:T(8,128)(2,1)} collective-permute-done((bf16[2,512,1536]{1,2,0:T(8,128)(2,1)}, bf16[2,512,1536]{1,2,0:T(8,128)(2,1)}, u32[]{:S(2)}, u32[]{:S(2)}) %collective-permute-start.1) | collective-permute-done | bytes 3145760 | tf_op jit(solution)/shard_map/ppermute | solution.py:14
  343.5 82.5 %collective-permute-done = bf16[2,512,1536]{1,2,0:T(8,128)(2,1)} collective-permute-done((bf16[2,512,1536]{1,2,0:T(8,128)(2,1)}, bf16[2,512,1536]{1,2,0:T(8,128)(2,1)}, u32[]{:S(2)}, u32[]{:S(2)}) %collective-permute-start) | collective-permute-done | bytes 3145760 | tf_op jit(solution)/shard_map/ppermute | solution.py:14
  431.7 6.9 %bitcast_reduce_fusion.1 = (f32[12,512]{1,0:T(8,128)S(1)}, f32[12,512,512]{1,2,0:T(8,128)}) fusion(pred[]{:T(512)S(6)} %and.11, bf16[512,12,128]{0,2,1:T(8,128)(2,1)S(1)} %bitcast.156, bf16[512,12,128]{0,2,1:T(8,128)(2,1)S(1)} %reshape.69), kind=kOutput, calls=%fused_computation.4 | convolution fusion | flops 814737408 | bytes 15753217 | tf_op jit(solution)/shard_map/qhd,khd->hqk/dot_general | solution.py:38
  444.3 7.8 %fusion.13 = f32[12,128,512]{1,2,0:T(8,128)} fusion(bf16[512,12,128]{0,2,1:T(8,128)(2,1)} %bitcast.162, f32[12,512,512]{1,2,0:T(8,128)} %get-tuple-element.24, f32[12,512]{1,0:T(8,128)S(1)} %get-tuple-element.10, pred[]{:T(512)S(6)} %and.11), kind=kOutput, calls=%fused_computation.23 | convolution fusion | flops 817889280 | bytes 17326080 | tf_op jit(solution)/shard_map/hqk,khd->qhd/dot_general | solution.py:51
  452.1 9.0 %fusion.5 = (f32[12,512]{1,0:T(8,128)S(1)}, f32[12,512]{1,0:T(8,128)S(1)}) fusion(f32[12,512,512]{1,2,0:T(8,128)S(1)} %get-tuple-element.28, f32[12,512]{1,0:T(8,128)S(1)} %get-tuple-element.11, pred[]{:T(512)S(6)} %and.10, f32[12,512]{1,0:T(8,128)S(1)} %get-tuple-element.10, f32[12,512,512]{1,2,0:T(8,128)} %get-tuple-element.24, pred[]{:T(512)S(6)} %and.11), kind=kLoop, calls=%fused_computation.16 | loop fusion | flops 25153536 | bytes 25264130 | tf_op jit(solution)/shard_map/reduce_sum | solution.py:50
  461.1 4.3 fusion.15
  465.4 3.4 fusion.9
  469.6 6.1 %fusion.35 = bf16[512,12,128]{2,0,1:T(8,128)(2,1)S(1)} fusion(f32[12,128,512]{1,2,0:T(8,128)S(1)} %copy-done.11, f32[12,128,512]{1,2,0:T(8,128)S(1)} %copy-done.12, f32[12,512,128]{2,1,0:T(8,128)S(1)} %copy-done.5, bf16[512,12,128]{0,2,1:T(8,128)(2,1)S(1)} %bitcast.160, f32[12,512,512]{1,2,0:T(8,128)S(1)} %get-tuple-element.22, ...), kind=kOutput, calls=%fused_computation.44 | convolution fusion | flops 824180736 | bytes 25288704 | tf_op jit(solution)/shard_map/hqk,khd->qhd/dot_general | solution.py:51
  478.3 3.6 all-to-all-start.3
  483.4 22.4 %all-to-all-done.3 = bf16[4,128,1536]{1,2,0:T(8,128)(2,1)S(1)} async-done(((bf16[4,128,1536]{1,2,0:T(8,128)(2,1)}), bf16[4,128,1536]{1,2,0:T(8,128)(2,1)S(1)}, u32[]{:S(2)}, u32[]{:S(2)}) %all-to-all-start.3) | async-done | bytes 1572896 | tf_op jit(solution)/shard_map/all_to_all | solution.py:70
  (55 shorter events, 44.2 us)
Async XLA Ops:
  0.0 129.2 %copy-start = (s32[64,3]{0,1:T(4,128)S(1)}, s32[64,3]{0,1:T(4,128)}, u32[]{:S(2)}) copy-start(s32[64,3]{0,1:T(4,128)} %param.10) | copy-start | bytes 2308
  0.0 9.4 %copy-start.6 = (bf16[128,6144]{1,0:T(8,128)(2,1)S(1)}, bf16[128,6144]{1,0:T(8,128)(2,1)}, u32[]{:S(2)}) copy-start(bf16[128,6144]{1,0:T(8,128)(2,1)} %param.8) | copy-start | bytes 4718596
  2.7 47.3 %all-to-all-start.1 = ((bf16[128,4,1536]{0,2,1:T(8,128)(2,1)}), bf16[128,4,1536]{0,2,1:T(8,128)(2,1)S(1)}, u32[]{:S(2)}, u32[]{:S(2)}) async-start(bf16[128,4,1536]{0,2,1:T(8,128)(2,1)} %bitcast.2), calls=%async_computation.1 | async-start | bytes 3145728 | tf_op jit(solution)/shard_map/all_to_all | solution.py:20
  50.0 44.4 %all-to-all-start.2 = ((bf16[128,4,1536]{0,2,1:T(8,128)(2,1)}), bf16[128,4,1536]{0,2,1:T(8,128)(2,1)S(1)}, u32[]{:S(2)}, u32[]{:S(2)}) async-start(bf16[128,4,1536]{0,2,1:T(8,128)(2,1)} %bitcast.157), calls=%async_computation.2 | async-start | bytes 3145728 | tf_op jit(solution)/shard_map/all_to_all | solution.py:21
  94.4 4.4 copy-start.3
  94.4 46.1 %all-to-all-start = ((bf16[128,4,1536]{0,2,1:T(8,128)(2,1)}), bf16[128,4,1536]{0,2,1:T(8,128)(2,1)}, u32[]{:S(2)}, u32[]{:S(2)}) async-start(bf16[128,4,1536]{0,2,1:T(8,128)(2,1)} %bitcast), calls=%async_computation | async-start | bytes 3145728 | tf_op jit(solution)/shard_map/all_to_all | solution.py:19
  117.8 2.8 copy-start.4
  121.8 218.4 %collective-permute-start.1 = (bf16[2,512,1536]{1,2,0:T(8,128)(2,1)}, bf16[2,512,1536]{1,2,0:T(8,128)(2,1)}, u32[]{:S(2)}, u32[]{:S(2)}) collective-permute-start(bf16[2,512,1536]{1,2,0:T(8,128)(2,1)} %constant_dynamic-update-slice_fusion), channel_id=1, source_target_pairs={{0,8},{4,12},{8,16},{12,20},{16,24},{20,28},{24,32},{28,36},{32,40... | collective-permute-start | bytes 9437192 | tf_op jit(solution)/shard_map/ppermute | solution.py:14
  125.3 300.7 %collective-permute-start = (bf16[2,512,1536]{1,2,0:T(8,128)(2,1)}, bf16[2,512,1536]{1,2,0:T(8,128)(2,1)}, u32[]{:S(2)}, u32[]{:S(2)}) collective-permute-start(bf16[2,512,1536]{1,2,0:T(8,128)(2,1)} %constant_dynamic-update-slice_fusion), channel_id=1, source_target_pairs={{0,4},{4,8},{8,12},{12,16},{16,20},{20,24},{24,28},{28,32},{32,36}... | collective-permute-start | bytes 9437192 | tf_op jit(solution)/shard_map/ppermute | solution.py:14
  135.8 302.7 %collective-permute-start.2 = (bf16[2,512,1536]{1,2,0:T(8,128)(2,1)}, bf16[2,512,1536]{1,2,0:T(8,128)(2,1)}, u32[]{:S(2)}, u32[]{:S(2)}) collective-permute-start(bf16[2,512,1536]{1,2,0:T(8,128)(2,1)} %constant_dynamic-update-slice_fusion), channel_id=1, source_target_pairs={{0,12},{4,16},{8,20},{12,24},{16,28},{20,32},{24,36},{28,40},{32,4... | collective-permute-start | bytes 9437192 | tf_op jit(solution)/shard_map/ppermute | solution.py:14
  151.5 7.9 %copy-start.2 = (bf16[512,12,128]{0,2,1:T(8,128)(2,1)S(1)}, bf16[512,12,128]{0,2,1:T(8,128)(2,1)}, u32[]{:S(2)}) copy-start(bf16[512,12,128]{0,2,1:T(8,128)(2,1)} %reshape_squeeze_stack.7) | copy-start | bytes 4718596
  452.1 9.0 %copy-start.8 = (bf16[1,512,1536]{1,2,0:T(8,128)(2,1)S(1)}, bf16[1,512,1536]{1,2,0:T(8,128)(2,1)}, u32[]{:S(2)}) copy-start(bf16[1,512,1536]{1,2,0:T(8,128)(2,1)} %get-tuple-element.14) | copy-start | bytes 4718596
  465.4 3.4 copy-start.5
  465.4 3.4 copy-start.7
  465.4 3.5 copy-start.11
  465.4 4.2 copy-start.12
  476.9 4.9 copy-start.10
  476.9 6.3 %copy-start.9 = (f32[8,6144]{1,0:T(8,128)S(1)}, f32[8,6144]{1,0:T(8,128)}, u32[]{:S(2)}) copy-start(f32[8,6144]{1,0:T(8,128)} %param.11) | copy-start | bytes 589828
  478.3 27.5 %all-to-all-start.3 = ((bf16[4,128,1536]{1,2,0:T(8,128)(2,1)}), bf16[4,128,1536]{1,2,0:T(8,128)(2,1)S(1)}, u32[]{:S(2)}, u32[]{:S(2)}) async-start(bf16[4,128,1536]{1,2,0:T(8,128)(2,1)} %copy.83), calls=%async_computation.3 | async-start | bytes 3145728 | tf_op jit(solution)/shard_map/all_to_all | solution.py:70
  483.2 25.1 %copy-start.1 = (s32[64,3]{0,1:T(4,128)S(1)}, s32[64,3]{0,1:T(4,128)}, u32[]{:S(2)}) copy-start(s32[64,3]{0,1:T(4,128)} %param.10) | copy-start | bytes 2308
where the time goes:
time: 509 us; the launch traced here: 508 us
  waiting for transfers between devices  347 us (68%)
  local copies, waits for them, and re-layouts  60.9 us (12%)
  matrix products  46.9 us (9%)
  starting transfers between devices  30.1 us (6%)
  other arithmetic  21 us (4%)
    ppermute x3, waiting for transfers between devices, shifted(): return lax.ppermute(x, axis, pairs)  248 us
    all_to_all x1, waiting for transfers between devices, shards(): lax.all_to_all(keys, 'seq', split_axis=1, concat_axis=0, tiled=True)  39 us
    all_to_all x1, waiting for transfers between devices, shards(): lax.all_to_all(values, 'seq', split_axis=1, concat_axis=0, tiled=True)  38.2 us
    dot_general x4, matrix products, shards(): jnp.einsum('hqk,khd->qhd', weights.astype(jnp.bfloat16), value_heads, pre...  27.2 us
    all_to_all x1, waiting for transfers between devices, shards(): lax.all_to_all(attended, 'seq', split_axis=0, concat_axis=1, tiled=True)  22.4 us
    dot_general x4, matrix products, shards(): jnp.einsum('qhd,khd->hqk', query_heads, key_heads, preferred_element_type...  19.7 us
    reduce_sum x3, other arithmetic, shards(): block_total = jnp.sum(weights, axis=-1)  19.2 us
    ppermute x3, starting transfers between devices, shifted(): return lax.ppermute(x, axis, pairs)  11.9 us
  transfers between devices with their start and end apart: 7, of which 5 were waited for; matrix products, arithmetic and copies ran while one was open for 16% of the time, Pallas kernels for 0%

commit v1 on v0

v1 whole, which is shorter than its diff:
```python
import functools

import jax
import jax.numpy as jnp
from jax import lax
from jax.experimental import pallas as pl
from jax.experimental.pallas import tpu as pltpu
from jax.sharding import PartitionSpec as P

HD = 128
WINDOW = 3
LEVELS = 8
ZLO = 4
SEQ = 4
RING = ZLO * SEQ
CTOK = 512
TOK = CTOK // SEQ
HEADS = 3
WIDTH = HEADS * HD
QROWS = 256
MESH = pl.DeviceIdType.MESH
PEERS = [(0, 1)] + [(r, b) for r in (1, 7, 2, 6, 3, 5, 4) for b in (0, 1)]


def block(i, size=HD):
    return pl.ds(pl.multiple_of(i * size, size), size)


def kernel(rings, q_ref, k_ref, v_ref, noise_ref, mask_ref, gate_ref, out_ref,
           qbuf, kbuf, vbuf, obuf, send, q_sem, k_sem, v_sem, halo_send, kh_sem, vh_sem, o_send, o_sem):
    group, seq = lax.axis_index("group"), lax.axis_index("seq")
    ring, zlo = group // ZLO, lax.rem(group, ZLO)
    core = lax.rem(seq, 2)
    z = (seq // 2) * ZLO + zlo

    def peer(r, b):
        z_there = lax.rem(z + r, 2 * ZLO)
        return lax.rem(z_there, ZLO), (z_there // ZLO) * 2 + lax.rem(core + b, 2)

    def device(place):
        return ring * ZLO + place[0], place[1]

    def heads_at(place):
        return (place[0] * SEQ + place[1]) * HEADS

    onward = lax.rem(ring + 1, rings) * ZLO + zlo, seq
    backward = lax.rem(ring + rings - 1, rings) * ZLO + zlo, seq

    barrier = pltpu.get_barrier_semaphore()
    for there in [device(peer(r, b)) for r, b in PEERS] + [onward, backward]:
        pl.semaphore_signal(barrier, inc=1, device_id=there, device_id_type=MESH)
    pl.semaphore_wait(barrier, len(PEERS) + 2)

    mine = heads_at((zlo, seq))
    place_q = zlo * SEQ + seq
    place_kv = place_q + WINDOW * SEQ

    def spread(src, buf, place, sem, send_sem, h):
        for r, b in PEERS:
            there = peer(r, b)
            pltpu.make_async_remote_copy(
                src_ref=src.at[:, block(heads_at(there) + h)],
                dst_ref=buf.at[h, block(place)],
                send_sem=send_sem,
                recv_sem=sem.at[h],
                device_id=device(there),
                device_id_type=MESH,
            ).start()
        pltpu.make_async_copy(src.at[:, block(mine + h)], buf.at[h, block(place)], sem.at[h]).start()

    @pl.loop(0, HEADS)
    def _(h):
        spread(k_ref, kbuf, place_kv, k_sem, send.at[0], h)
        spread(v_ref, vbuf, place_kv, v_sem, send.at[1], h)

    @pl.loop(0, HEADS)
    def _(h):
        spread(q_ref, qbuf, place_q, q_sem, send.at[2], h)

    def wait_bytes(part, sem):
        pltpu.make_async_copy(part, part, sem).wait()

    def halo(buf, sem, send_sem, h):
        return pltpu.make_async_remote_copy(
            src_ref=buf.at[h, pl.ds(ZLO * CTOK, WINDOW * CTOK)],
            dst_ref=buf.at[h, pl.ds(0, WINDOW * CTOK)],
            send_sem=send_sem.at[h],
            recv_sem=sem.at[h],
            device_id=onward,
            device_id_type=MESH,
        )

    @pl.loop(0, HEADS)
    def _(h):
        for i, (buf, sem, h_sem) in enumerate(((kbuf, k_sem, kh_sem), (vbuf, v_sem, vh_sem))):
            wait_bytes(buf.at[h, pl.ds(WINDOW * CTOK, ZLO * CTOK)], sem.at[h])
            halo(buf, h_sem, halo_send.at[i], h).start()

    factor = HD ** (-0.5) * 1.4426950408889634

    @pl.loop(0, HEADS)
    def _(h):
        wait_bytes(qbuf.at[h], q_sem.at[h])
        halo(kbuf, kh_sem, halo_send.at[0], h).wait_recv()
        halo(vbuf, vh_sem, halo_send.at[1], h).wait_recv()

        @pl.loop(0, ZLO)
        def _(step):
            g = lax.rem(zlo + step, ZLO)
            c = ring * ZLO + g
            seen = [
                (c - k >= 0) & (mask_ref[c, k - 1] == 1) if k else None for k in range(WINDOW, -1, -1)
            ]
            level = noise_ref[c]
            table = gate_ref[:, block(mine + h)]
            pick = lax.broadcasted_iota(jnp.int32, (LEVELS, HD), 0) == level
            gate = jnp.sum(jnp.where(pick, table, 0.0), axis=0, keepdims=True)

            @pl.loop(0, CTOK // QROWS)
            def _(part):
                rows = block(g * (CTOK // QROWS) + part, QROWS)
                q = qbuf[h, rows, :]
                scores, top = [], None
                for k in range(WINDOW + 1):
                    s = lax.dot_general(
                        q, kbuf[h, block(g + k, CTOK), :], (((1,), (1,)), ((), ())),
                        preferred_element_type=jnp.float32,
                    )
                    high = jnp.max(s, axis=1, keepdims=True)
                    if seen[k] is not None:
                        high = jnp.where(seen[k], high, -1e30)
                    top = high if top is None else jnp.maximum(top, high)
                    scores.append(s)
                top = top * factor
                total, summed = None, None
                for k in range(WINDOW + 1):
                    base = top if seen[k] is None else jnp.where(seen[k], top, 1e30)
                    weight = jnp.exp2(scores[k] * factor - base)
                    t = jnp.sum(weight, axis=1, keepdims=True)
                    o = jnp.dot(
                        weight.astype(jnp.bfloat16), vbuf[h, block(g + k, CTOK), :],
                        preferred_element_type=jnp.float32,
                    )
                    total = t if total is None else total + t
                    summed = o if summed is None else summed + o
                attended = (summed / total).astype(jnp.bfloat16)
                obuf[h, rows, :] = (attended.astype(jnp.float32) * gate).astype(jnp.bfloat16)

            for t in range(SEQ):
                s_there = lax.rem(seq + t, SEQ)
                src = obuf.at[h, block(g * SEQ + s_there)]
                dst = out_ref.at[:, block(mine + h)]

                def away():
                    pltpu.make_async_remote_copy(
                        src_ref=src, dst_ref=dst, send_sem=o_send, recv_sem=o_sem,
                        device_id=(c, s_there), device_id_type=MESH,
                    ).start()

                def here():
                    pltpu.make_async_copy(src, dst, o_sem).start()

                if t:
                    away()
                else:
                    pl.when(step == 0)(here)
                    pl.when(step != 0)(away)

    sent = pl.ds(0, (RING - 1) * TOK)
    wait_bytes(kbuf.at[:, sent], send.at[0])
    wait_bytes(vbuf.at[:, sent], send.at[1])
    wait_bytes(qbuf.at[:, sent], send.at[2])

    @pl.loop(0, HEADS)
    def _(h):
        halo(kbuf, kh_sem, halo_send.at[0], h).wait_send()
        halo(vbuf, vh_sem, halo_send.at[1], h).wait_send()

    wait_bytes(obuf.at[:, sent], o_send)
    wait_bytes(out_ref, o_sem)


def shards(rings, queries, keys, values, noise_level, block_mask, gate_table):
    anywhere = pl.BlockSpec(memory_space=pl.ANY)
    scalars = pl.BlockSpec(memory_space=pltpu.SMEM)
    dma = pltpu.SemaphoreType.DMA
    return pl.pallas_call(
        functools.partial(kernel, rings),
        out_shape=jax.ShapeDtypeStruct(queries.shape, queries.dtype),
        in_specs=[anywhere, anywhere, anywhere, scalars, scalars, pl.BlockSpec(memory_space=pltpu.VMEM)],
        out_specs=anywhere,
        scratch_shapes=[
            pltpu.VMEM((HEADS, ZLO * CTOK, HD), jnp.bfloat16),
            pltpu.VMEM((HEADS, (ZLO + WINDOW) * CTOK, HD), jnp.bfloat16),
            pltpu.VMEM((HEADS, (ZLO + WINDOW) * CTOK, HD), jnp.bfloat16),
            pltpu.VMEM((HEADS, ZLO * CTOK, HD), jnp.bfloat16),
            dma((3,)), dma((HEADS,)), dma((HEADS,)), dma((HEADS,)),
            dma((2, HEADS)), dma((HEADS,)), dma((HEADS,)), dma, dma,
        ],
        compiler_params=pltpu.CompilerParams(
            collective_id=0, has_side_effects=True, vmem_limit_bytes=48 * 2**20
        ),
    )(queries, keys, values, noise_level, block_mask, gate_table)


def solution(mesh):
    placed = (
        P(("group", "seq"), None),
        P(("group", "seq"), None),
        P(("group", "seq"), None),
        P(),
        P(),
        P(),
    )
    return jax.shard_map(
        functools.partial(shards, mesh.shape["group"] // ZLO),
        mesh=mesh, in_specs=placed, out_specs=P(("group", "seq"), None), check_vma=False,
    )
```

time: 509 us -> 156 us (0.31)
  the two profiles are of different devices: /device:TPU:64 before, /device:TPU:1 now
where the time goes in v1:
time: 156 us
  Pallas kernels  149 us (96%)
  local copies, waits for them, and re-layouts  6.31 us (4%)
    pallas_call x1, Pallas kernels, shards(): pl.pallas_call(functools.partial(kernel, rings), out_shape=jax.ShapeDtype...  149 us
    unnamed x10, local copies, waits for them, and re-layouts  6.31 us

profile of v1, /device:TPU:1, one launch (start us, length us, event | category | flops | bytes accessed | tf_op | source)
XLA Modules:
  0.0 155.7 jit_solution(2301259980595188668)
XLA Ops:
  0.0 0.8 copy.7.mask_ref
  0.8 0.0 copy-start
  0.8 1.4 copy-done
  2.2 0.0 copy-start.1
  2.2 1.4 copy-done.1
  3.6 0.0 copy-start.2
  3.6 0.9 copy-done.2
  4.5 0.0 copy-start.3
  4.5 0.7 copy-done.3
  5.2 149.4 %shard_map.64 = bf16[128,6144]{1,0:T(8,128)(2,1)S(1)} custom-call(bf16[128,6144]{1,0:T(8,128)(2,1)S(1)} %copy-done, bf16[128,6144]{1,0:T(8,128)(2,1)S(1)} %copy-done.1, bf16[128,6144]{1,0:T(8,128)(2,1)} %v_ref.1, s32[64]{0:T(128)S(1)} %copy-done.3, s32[64,3]{1,0:T(8,128)S(1)} %copy.7.mask_ref, f32[8,6144]{1,0:T(8,128)S(1)} %copy-done.2), custom_call_target="tpu_custom_call" | custom-call | tf_op jit(solution)/shard_map/pallas_call | solution.py:187
  154.6 1.1 copy.9
Async XLA Ops:
  0.8 1.4 copy-start
  2.2 1.4 copy-start.1
  3.6 0.9 copy-start.2
  4.5 0.7 copy-start.3

commit v2 on v1

--- a/solution.py
+++ b/solution.py
@@ -19,15 +19,15 @@
 WIDTH = HEADS * HD
 QROWS = 256
 MESH = pl.DeviceIdType.MESH
-PEERS = [(0, 1)] + [(r, b) for r in (1, 7, 2, 6, 3, 5, 4) for b in (0, 1)]
+PEERS = [(r, b) for r in (4, 3, 5, 2, 6, 1, 7) for b in (0, 1)] + [(0, 1)]
 
 
 def block(i, size=HD):
     return pl.ds(pl.multiple_of(i * size, size), size)
 
 
-def kernel(rings, q_ref, k_ref, v_ref, noise_ref, mask_ref, gate_ref, out_ref,
-           qbuf, kbuf, vbuf, obuf, send, q_sem, k_sem, v_sem, halo_send, kh_sem, vh_sem, o_send, o_sem):
+def kernel(rings, q_ref, k_ref, v_ref, noise_any, mask_any, gate_any, out_ref,
+           noise_ref, mask_ref, gate_ref, small_sem, qbuf, kbuf, vbuf, obuf, send, q_sem, k_sem, v_sem, halo_send, kh_sem, vh_sem, o_send, o_sem):
     group, seq = lax.axis_index("group"), lax.axis_index("seq")
     ring, zlo = group // ZLO, lax.rem(group, ZLO)
     core = lax.rem(seq, 2)
@@ -49,11 +49,24 @@
     barrier = pltpu.get_barrier_semaphore()
     for there in [device(peer(r, b)) for r, b in PEERS] + [onward, backward]:
         pl.semaphore_signal(barrier, inc=1, device_id=there, device_id_type=MESH)
-    pl.semaphore_wait(barrier, len(PEERS) + 2)
-
     mine = heads_at((zlo, seq))
+    small = [
+        pltpu.make_async_copy(noise_any, noise_ref, small_sem.at[0]),
+        pltpu.make_async_copy(mask_any, mask_ref, small_sem.at[1]),
+        pltpu.make_async_copy(gate_any.at[:, block(mine // HEADS, WIDTH)], gate_ref, small_sem.at[2]),
+    ]
+    for copy in small:
+        copy.start()
     place_q = zlo * SEQ + seq
     place_kv = place_q + WINDOW * SEQ
+
+    @pl.loop(0, HEADS)
+    def _(h):
+        for src, buf, place, sem in ((k_ref, kbuf, place_kv, k_sem), (v_ref, vbuf, place_kv, v_sem), (q_ref, qbuf, place_q, q_sem)):
+            pltpu.make_async_copy(src.at[:, block(mine + h)], buf.at[h, block(place)], sem.at[h]).start()
+
+    pl.semaphore_wait(barrier, len(PEERS) + 2)
+
 
     def spread(src, buf, place, sem, send_sem, h):
         for r, b in PEERS:
@@ -66,7 +79,6 @@
                 device_id=device(there),
                 device_id_type=MESH,
             ).start()
-        pltpu.make_async_copy(src.at[:, block(mine + h)], buf.at[h, block(place)], sem.at[h]).start()
 
     @pl.loop(0, HEADS)
     def _(h):
@@ -96,6 +108,8 @@
             wait_bytes(buf.at[h, pl.ds(WINDOW * CTOK, ZLO * CTOK)], sem.at[h])
             halo(buf, h_sem, halo_send.at[i], h).start()
 
+    for copy in small:
+        copy.wait()
     factor = HD ** (-0.5) * 1.4426950408889634
 
     @pl.loop(0, HEADS)
@@ -106,13 +120,14 @@
 
         @pl.loop(0, ZLO)
         def _(step):
-            g = lax.rem(zlo + step, ZLO)
+            turn = lax.rem(2 * step + 1 - step // 2, ZLO)
+            g = lax.rem(zlo + turn, ZLO)
             c = ring * ZLO + g
             seen = [
-                (c - k >= 0) & (mask_ref[c, k - 1] == 1) if k else None for k in range(WINDOW, -1, -1)
+                (c - k >= 0) & (mask_ref[k - 1, c] == 1) if k else None for k in range(WINDOW, -1, -1)
             ]
             level = noise_ref[c]
-            table = gate_ref[:, block(mine + h)]
+            table = gate_ref[:, block(h)]
             pick = lax.broadcasted_iota(jnp.int32, (LEVELS, HD), 0) == level
             gate = jnp.sum(jnp.where(pick, table, 0.0), axis=0, keepdims=True)
 
@@ -163,8 +178,8 @@
                 if t:
                     away()
                 else:
-                    pl.when(step == 0)(here)
-                    pl.when(step != 0)(away)
+                    pl.when(turn == 0)(here)
+                    pl.when(turn != 0)(away)
 
     sent = pl.ds(0, (RING - 1) * TOK)
     wait_bytes(kbuf.at[:, sent], send.at[0])
@@ -182,14 +197,17 @@
 
 def shards(rings, queries, keys, values, noise_level, block_mask, gate_table):
     anywhere = pl.BlockSpec(memory_space=pl.ANY)
-    scalars = pl.BlockSpec(memory_space=pltpu.SMEM)
     dma = pltpu.SemaphoreType.DMA
     return pl.pallas_call(
         functools.partial(kernel, rings),
-        out_shape=jax.ShapeDtypeStruct(queries.shape, queries.dtype),
-        in_specs=[anywhere, anywhere, anywhere, scalars, scalars, pl.BlockSpec(memory_space=pltpu.VMEM)],
+        out_shape=pltpu.VMEM(queries.shape, queries.dtype),
+        in_specs=[anywhere] * 6,
         out_specs=anywhere,
         scratch_shapes=[
+            pltpu.SMEM(noise_level.shape, jnp.int32),
+            pltpu.SMEM(block_mask.shape[::-1], jnp.int32),
+            pltpu.VMEM((LEVELS, WIDTH), jnp.float32),
+            dma((3,)),
             pltpu.VMEM((HEADS, ZLO * CTOK, HD), jnp.bfloat16),
             pltpu.VMEM((HEADS, (ZLO + WINDOW) * CTOK, HD), jnp.bfloat16),
             pltpu.VMEM((HEADS, (ZLO + WINDOW) * CTOK, HD), jnp.bfloat16),
@@ -198,9 +216,9 @@
             dma((2, HEADS)), dma((HEADS,)), dma((HEADS,)), dma, dma,
         ],
         compiler_params=pltpu.CompilerParams(
-            collective_id=0, has_side_effects=True, vmem_limit_bytes=48 * 2**20
+            collective_id=0, has_side_effects=True, vmem_limit_bytes=40 * 2**20
         ),
-    )(queries, keys, values, noise_level, block_mask, gate_table)
+    )(*(pltpu.with_memory_space_constraint(x, pltpu.HBM) for x in (queries, keys, values, noise_level, block_mask.T, gate_table)))
 
 
 def solution(mesh):

time: 156 us -> 149 us (0.955)
  local copies, waits for them, and re-layouts: 6.31 us -> 1.15 us
    unnamed x10 -> x1, local copies, waits for them, and re-layouts: 6.31 us -> 1.15 us
    pallas_call x1, Pallas kernels: 149 us -> 148 us  [shards(): pl.pallas_call(functools.partial(kernel, rings), out_shape=pltpu.VMEM(que...]
where the time goes in v2:
time: 149 us
  Pallas kernels  148 us (99%)
    pallas_call x1, Pallas kernels, shards(): pl.pallas_call(functools.partial(kernel, rings), out_shape=pltpu.VMEM(que...  148 us

profile of v2, /device:TPU:1, one launch (start us, length us, event | category | flops | bytes accessed | tf_op | source)
XLA Modules:
  0.0 148.9 jit_solution(17790587857793245211)
XLA Ops:
  0.0 147.7 %shard_map.64 = bf16[128,6144]{1,0:T(8,128)(2,1)S(1)} custom-call(bf16[128,6144]{1,0:T(8,128)(2,1)} %q_ref.1, bf16[128,6144]{1,0:T(8,128)(2,1)} %k_ref.1, bf16[128,6144]{1,0:T(8,128)(2,1)} %v_ref.1, s32[64]{0:T(128)} %noise_any.1, s32[3,64]{1,0:T(4,128)} %bitcast.1, f32[8,6144]{1,0:T(8,128)} %gate_any.1), custom_call_target="tpu_custom_call" | custom-call | tf_op jit(solution)/shard_map/pallas_call | solution.py:201
  147.7 1.1 copy.8

commit v3 on v2

--- a/solution.py
+++ b/solution.py
@@ -17,17 +17,35 @@
 TOK = CTOK // SEQ
 HEADS = 3
 WIDTH = HEADS * HD
-QROWS = 256
 MESH = pl.DeviceIdType.MESH
 PEERS = [(r, b) for r in (4, 3, 5, 2, 6, 1, 7) for b in (0, 1)] + [(0, 1)]
 
 
+ORDER = (
+    (1, 2, 3, 0),
+    (0, 0, 0, 2),
+    (3, 1, 1, 3),
+    (5, 6, 7, 4),
+    (2, 3, 2, 1),
+    (6, 7, 4, 5),
+    (7, 4, 5, 6),
+    (4, 5, 6, 7),
+)
+
+
+def choose(i, options):
+    result = options[-1]
+    for j, option in enumerate(options[:-1]):
+        result = jnp.where(i == j, option, result)
+    return result
+
+
 def block(i, size=HD):
     return pl.ds(pl.multiple_of(i * size, size), size)
 
 
 def kernel(rings, q_ref, k_ref, v_ref, noise_any, mask_any, gate_any, out_ref,
-           noise_ref, mask_ref, gate_ref, small_sem, qbuf, kbuf, vbuf, obuf, send, q_sem, k_sem, v_sem, halo_send, kh_sem, vh_sem, o_send, o_sem):
+           noise_ref, mask_ref, gate_ref, small_sem, qbuf, kbuf, vbuf, obuf, send, q_sem, k_sem, v_sem, go_sem, halo_send, kh_sem, vh_sem, o_send, o_sem):
     group, seq = lax.axis_index("group"), lax.axis_index("seq")
     ring, zlo = group // ZLO, lax.rem(group, ZLO)
     core = lax.rem(seq, 2)
@@ -43,12 +61,18 @@
     def heads_at(place):
         return (place[0] * SEQ + place[1]) * HEADS
 
-    onward = lax.rem(ring + 1, rings) * ZLO + zlo, seq
-    backward = lax.rem(ring + rings - 1, rings) * ZLO + zlo, seq
+    hands_on, is_handed = ring < rings - 1, ring > 0
+    onward = jnp.minimum(ring + 1, rings - 1) * ZLO + zlo, seq
+    backward = jnp.maximum(ring - 1, 0) * ZLO + zlo, seq
 
     barrier = pltpu.get_barrier_semaphore()
-    for there in [device(peer(r, b)) for r, b in PEERS] + [onward, backward]:
-        pl.semaphore_signal(barrier, inc=1, device_id=there, device_id_type=MESH)
+
+    @pl.when(hands_on)
+    def _():
+        pl.semaphore_signal(barrier, inc=1, device_id=onward, device_id_type=MESH)
+
+    for r, b in PEERS:
+        pl.semaphore_signal(barrier, inc=1, device_id=device(peer(r, b)), device_id_type=MESH)
     mine = heads_at((zlo, seq))
     small = [
         pltpu.make_async_copy(noise_any, noise_ref, small_sem.at[0]),
@@ -65,7 +89,7 @@
         for src, buf, place, sem in ((k_ref, kbuf, place_kv, k_sem), (v_ref, vbuf, place_kv, v_sem), (q_ref, qbuf, place_q, q_sem)):
             pltpu.make_async_copy(src.at[:, block(mine + h)], buf.at[h, block(place)], sem.at[h]).start()
 
-    pl.semaphore_wait(barrier, len(PEERS) + 2)
+    pl.semaphore_wait(barrier, len(PEERS) + is_handed.astype(jnp.int32))
 
 
     def spread(src, buf, place, sem, send_sem, h):
@@ -89,6 +113,20 @@
     def _(h):
         spread(q_ref, qbuf, place_q, q_sem, send.at[2], h)
 
+    @pl.when(is_handed)
+    def _():
+        pl.semaphore_signal(go_sem, inc=1, device_id=backward, device_id_type=MESH)
+
+    @pl.when(jnp.logical_not(is_handed))
+    def _():
+        nothing = jnp.zeros((HEADS, WINDOW * CTOK, HD), jnp.bfloat16)
+        kbuf[:, pl.ds(0, WINDOW * CTOK), :] = nothing
+        vbuf[:, pl.ds(0, WINDOW * CTOK), :] = nothing
+
+    @pl.when(hands_on)
+    def _():
+        pl.semaphore_wait(go_sem, 1)
+
     def wait_bytes(part, sem):
         pltpu.make_async_copy(part, part, sem).wait()
 
@@ -106,7 +144,7 @@
     def _(h):
         for i, (buf, sem, h_sem) in enumerate(((kbuf, k_sem, kh_sem), (vbuf, v_sem, vh_sem))):
             wait_bytes(buf.at[h, pl.ds(WINDOW * CTOK, ZLO * CTOK)], sem.at[h])
-            halo(buf, h_sem, halo_send.at[i], h).start()
+            pl.when(hands_on)(halo(buf, h_sem, halo_send.at[i], h).start)
 
     for copy in small:
         copy.wait()
@@ -115,13 +153,13 @@
     @pl.loop(0, HEADS)
     def _(h):
         wait_bytes(qbuf.at[h], q_sem.at[h])
-        halo(kbuf, kh_sem, halo_send.at[0], h).wait_recv()
-        halo(vbuf, vh_sem, halo_send.at[1], h).wait_recv()
-
-        @pl.loop(0, ZLO)
+        pl.when(is_handed)(halo(kbuf, kh_sem, halo_send.at[0], h).wait_recv)
+        pl.when(is_handed)(halo(vbuf, vh_sem, halo_send.at[1], h).wait_recv)
+
+        @pl.loop(0, 2 * ZLO)
         def _(step):
-            turn = lax.rem(2 * step + 1 - step // 2, ZLO)
-            g = lax.rem(zlo + turn, ZLO)
+            z_there = choose(step, [choose(zlo, column) for column in ORDER])
+            g, half = lax.rem(z_there, ZLO), z_there // ZLO
             c = ring * ZLO + g
             seen = [
                 (c - k >= 0) & (mask_ref[k - 1, c] == 1) if k else None for k in range(WINDOW, -1, -1)
@@ -131,38 +169,36 @@
             pick = lax.broadcasted_iota(jnp.int32, (LEVELS, HD), 0) == level
             gate = jnp.sum(jnp.where(pick, table, 0.0), axis=0, keepdims=True)
 
-            @pl.loop(0, CTOK // QROWS)
-            def _(part):
-                rows = block(g * (CTOK // QROWS) + part, QROWS)
-                q = qbuf[h, rows, :]
-                scores, top = [], None
-                for k in range(WINDOW + 1):
-                    s = lax.dot_general(
-                        q, kbuf[h, block(g + k, CTOK), :], (((1,), (1,)), ((), ())),
-                        preferred_element_type=jnp.float32,
-                    )
-                    high = jnp.max(s, axis=1, keepdims=True)
-                    if seen[k] is not None:
-                        high = jnp.where(seen[k], high, -1e30)
-                    top = high if top is None else jnp.maximum(top, high)
-                    scores.append(s)
-                top = top * factor
-                total, summed = None, None
-                for k in range(WINDOW + 1):
-                    base = top if seen[k] is None else jnp.where(seen[k], top, 1e30)
-                    weight = jnp.exp2(scores[k] * factor - base)
-                    t = jnp.sum(weight, axis=1, keepdims=True)
-                    o = jnp.dot(
-                        weight.astype(jnp.bfloat16), vbuf[h, block(g + k, CTOK), :],
-                        preferred_element_type=jnp.float32,
-                    )
-                    total = t if total is None else total + t
-                    summed = o if summed is None else summed + o
-                attended = (summed / total).astype(jnp.bfloat16)
-                obuf[h, rows, :] = (attended.astype(jnp.float32) * gate).astype(jnp.bfloat16)
-
-            for t in range(SEQ):
-                s_there = lax.rem(seq + t, SEQ)
+            rows = block(g * 2 + half, CTOK // 2)
+            q = qbuf[h, rows, :]
+            scores, top = [], None
+            for k in range(WINDOW + 1):
+                s = lax.dot_general(
+                    q, kbuf[h, block(g + k, CTOK), :], (((1,), (1,)), ((), ())),
+                    preferred_element_type=jnp.float32,
+                )
+                high = jnp.max(s, axis=1, keepdims=True)
+                if seen[k] is not None:
+                    high = jnp.where(seen[k], high, -1e30)
+                top = high if top is None else jnp.maximum(top, high)
+                scores.append(s)
+            top = top * factor
+            total, summed = None, None
+            for k in range(WINDOW + 1):
+                base = top if seen[k] is None else jnp.where(seen[k], top, 1e30)
+                weight = jnp.exp2(scores[k] * factor - base)
+                t = jnp.sum(weight, axis=1, keepdims=True)
+                o = jnp.dot(
+                    weight.astype(jnp.bfloat16), vbuf[h, block(g + k, CTOK), :],
+                    preferred_element_type=jnp.float32,
+                )
+                total = t if total is None else total + t
+                summed = o if summed is None else summed + o
+            attended = (summed / total).astype(jnp.bfloat16)
+            obuf[h, rows, :] = (attended.astype(jnp.float32) * gate).astype(jnp.bfloat16)
+
+            for t in range(2):
+                s_there = half * 2 + lax.rem(core + t, 2)
                 src = obuf.at[h, block(g * SEQ + s_there)]
                 dst = out_ref.at[:, block(mine + h)]
 
@@ -178,8 +214,8 @@
                 if t:
                     away()
                 else:
-                    pl.when(turn == 0)(here)
-                    pl.when(turn != 0)(away)
+                    pl.when(z_there == z)(here)
+                    pl.when(z_there != z)(away)
 
     sent = pl.ds(0, (RING - 1) * TOK)
     wait_bytes(kbuf.at[:, sent], send.at[0])
@@ -188,8 +224,8 @@
 
     @pl.loop(0, HEADS)
     def _(h):
-        halo(kbuf, kh_sem, halo_send.at[0], h).wait_send()
-        halo(vbuf, vh_sem, halo_send.at[1], h).wait_send()
+        pl.when(hands_on)(halo(kbuf, kh_sem, halo_send.at[0], h).wait_send)
+        pl.when(hands_on)(halo(vbuf, vh_sem, halo_send.at[1], h).wait_send)
 
     wait_bytes(obuf.at[:, sent], o_send)
     wait_bytes(out_ref, o_sem)
@@ -213,6 +249,7 @@
             pltpu.VMEM((HEADS, (ZLO + WINDOW) * CTOK, HD), jnp.bfloat16),
             pltpu.VMEM((HEADS, ZLO * CTOK, HD), jnp.bfloat16),
             dma((3,)), dma((HEADS,)), dma((HEADS,)), dma((HEADS,)),
+            pltpu.SemaphoreType.REGULAR,
             dma((2, HEADS)), dma((HEADS,)), dma((HEADS,)), dma, dma,
         ],
         compiler_params=pltpu.CompilerParams(

time: 149 us -> 146 us (0.980)
  the two profiles are of different devices: /device:TPU:1 before, /device:TPU:71 now
where the time goes in v3:
time: 146 us
  Pallas kernels  144 us (99%)
    pallas_call x1, Pallas kernels, shards(): pl.pallas_call(functools.partial(kernel, rings), out_shape=pltpu.VMEM(que...  144 us

profile of v3, /device:TPU:71, one launch (start us, length us, event | category | flops | bytes accessed | tf_op | source)
XLA Modules:
  0.0 145.6 jit_solution(2205984294040028590)
XLA Ops:
  0.0 144.4 %shard_map.64 = bf16[128,6144]{1,0:T(8,128)(2,1)S(1)} custom-call(bf16[128,6144]{1,0:T(8,128)(2,1)} %q_ref.1, bf16[128,6144]{1,0:T(8,128)(2,1)} %k_ref.1, bf16[128,6144]{1,0:T(8,128)(2,1)} %v_ref.1, s32[64]{0:T(128)} %noise_any.1, s32[3,64]{1,0:T(4,128)} %bitcast.1, f32[8,6144]{1,0:T(8,128)} %gate_any.1), custom_call_target="tpu_custom_call" | custom-call | tf_op jit(solution)/shard_map/pallas_call | solution.py:237
  144.4 1.1 copy.8

commit v4 on v3

--- a/solution.py
+++ b/solution.py
@@ -13,6 +13,7 @@
 ZLO = 4
 SEQ = 4
 RING = ZLO * SEQ
+ROW = 4
 CTOK = 512
 TOK = CTOK // SEQ
 HEADS = 3
@@ -22,11 +23,11 @@
 
 
 ORDER = (
-    (1, 2, 3, 0),
-    (0, 0, 0, 2),
-    (3, 1, 1, 3),
+    (1, 0, 0, 1),
+    (2, 2, 1, 0),
+    (0, 1, 2, 2),
     (5, 6, 7, 4),
-    (2, 3, 2, 1),
+    (3, 3, 3, 3),
     (6, 7, 4, 5),
     (7, 4, 5, 6),
     (4, 5, 6, 7),
@@ -62,14 +63,21 @@
         return (place[0] * SEQ + place[1]) * HEADS
 
     hands_on, is_handed = ring < rings - 1, ring > 0
+    starts_row, ends_row = lax.rem(ring, ROW) == 0, lax.rem(ring, ROW) == ROW - 1
+    waits_behind, leaves_behind = is_handed & jnp.logical_not(starts_row), is_handed & starts_row
+    waits_ahead, leaves_ahead = hands_on & ends_row, hands_on & jnp.logical_not(ends_row)
     onward = jnp.minimum(ring + 1, rings - 1) * ZLO + zlo, seq
     backward = jnp.maximum(ring - 1, 0) * ZLO + zlo, seq
 
     barrier = pltpu.get_barrier_semaphore()
 
-    @pl.when(hands_on)
+    @pl.when(leaves_ahead)
     def _():
         pl.semaphore_signal(barrier, inc=1, device_id=onward, device_id_type=MESH)
+
+    @pl.when(leaves_behind)
+    def _():
+        pl.semaphore_signal(barrier, inc=1, device_id=backward, device_id_type=MESH)
 
     for r, b in PEERS:
         pl.semaphore_signal(barrier, inc=1, device_id=device(peer(r, b)), device_id_type=MESH)
@@ -89,7 +97,7 @@
         for src, buf, place, sem in ((k_ref, kbuf, place_kv, k_sem), (v_ref, vbuf, place_kv, v_sem), (q_ref, qbuf, place_q, q_sem)):
             pltpu.make_async_copy(src.at[:, block(mine + h)], buf.at[h, block(place)], sem.at[h]).start()
 
-    pl.semaphore_wait(barrier, len(PEERS) + is_handed.astype(jnp.int32))
+    pl.semaphore_wait(barrier, len(PEERS) + waits_behind.astype(jnp.int32) + waits_ahead.astype(jnp.int32))
 
 
     def spread(src, buf, place, sem, send_sem, h):
@@ -113,7 +121,7 @@
     def _(h):
         spread(q_ref, qbuf, place_q, q_sem, send.at[2], h)
 
-    @pl.when(is_handed)
+    @pl.when(waits_behind)
     def _():
         pl.semaphore_signal(go_sem, inc=1, device_id=backward, device_id_type=MESH)
 
@@ -123,7 +131,7 @@
         kbuf[:, pl.ds(0, WINDOW * CTOK), :] = nothing
         vbuf[:, pl.ds(0, WINDOW * CTOK), :] = nothing
 
-    @pl.when(hands_on)
+    @pl.when(leaves_ahead)
     def _():
         pl.semaphore_wait(go_sem, 1)
 

time: 146 us -> 145 us (level)
  the two profiles are of different devices: /device:TPU:71 before, /device:TPU:1 now
where the time goes in v4:
time: 145 us
  Pallas kernels  144 us (99%)
    pallas_call x1, Pallas kernels, shards(): pl.pallas_call(functools.partial(kernel, rings), out_shape=pltpu.VMEM(que...  144 us

profile of v4, /device:TPU:1, one launch (start us, length us, event | category | flops | bytes accessed | tf_op | source)
XLA Modules:
  0.0 144.8 jit_solution(5136020853642677148)
XLA Ops:
  0.0 143.7 %shard_map.64 = bf16[128,6144]{1,0:T(8,128)(2,1)S(1)} custom-call(bf16[128,6144]{1,0:T(8,128)(2,1)} %q_ref.1, bf16[128,6144]{1,0:T(8,128)(2,1)} %k_ref.1, bf16[128,6144]{1,0:T(8,128)(2,1)} %v_ref.1, s32[64]{0:T(128)} %noise_any.1, s32[3,64]{1,0:T(4,128)} %bitcast.1, f32[8,6144]{1,0:T(8,128)} %gate_any.1), custom_call_target="tpu_custom_call" | custom-call | tf_op jit(solution)/shard_map/pallas_call | solution.py:245
  143.7 1.1 copy.8

commit v5 on v4

--- a/solution.py
+++ b/solution.py
@@ -19,7 +19,7 @@
 HEADS = 3
 WIDTH = HEADS * HD
 MESH = pl.DeviceIdType.MESH
-PEERS = [(r, b) for r in (4, 3, 5, 2, 6, 1, 7) for b in (0, 1)] + [(0, 1)]
+PEERS = [(r, b) for r in (1, 7, 2, 6, 3, 5, 4) for b in (0, 1)] + [(0, 1)]
 
 
 ORDER = (
@@ -206,7 +206,7 @@
             obuf[h, rows, :] = (attended.astype(jnp.float32) * gate).astype(jnp.bfloat16)
 
             for t in range(2):
-                s_there = half * 2 + lax.rem(core + t, 2)
+                s_there = half * 2 + 1 - t
                 src = obuf.at[h, block(g * SEQ + s_there)]
                 dst = out_ref.at[:, block(mine + h)]
 
@@ -219,11 +219,9 @@
                 def here():
                     pltpu.make_async_copy(src, dst, o_sem).start()
 
-                if t:
-                    away()
-                else:
-                    pl.when(z_there == z)(here)
-                    pl.when(z_there != z)(away)
+                own = (z_there == z) & (core == 1 - t)
+                pl.when(own)(here)
+                pl.when(jnp.logical_not(own))(away)
 
     sent = pl.ds(0, (RING - 1) * TOK)
     wait_bytes(kbuf.at[:, sent], send.at[0])

time: 145 us -> 145 us (level)
  no operation moved by 1% of the time
where the time goes in v5:
time: 145 us
  Pallas kernels  143 us (99%)
    pallas_call x1, Pallas kernels, shards(): pl.pallas_call(functools.partial(kernel, rings), out_shape=pltpu.VMEM(que...  143 us

profile of v5, /device:TPU:1, one launch (start us, length us, event | category | flops | bytes accessed | tf_op | source)
XLA Modules:
  0.0 144.6 jit_solution(16798334660593914177)
XLA Ops:
  0.0 143.4 %shard_map.64 = bf16[128,6144]{1,0:T(8,128)(2,1)S(1)} custom-call(bf16[128,6144]{1,0:T(8,128)(2,1)} %q_ref.1, bf16[128,6144]{1,0:T(8,128)(2,1)} %k_ref.1, bf16[128,6144]{1,0:T(8,128)(2,1)} %v_ref.1, s32[64]{0:T(128)} %noise_any.1, s32[3,64]{1,0:T(4,128)} %bitcast.1, f32[8,6144]{1,0:T(8,128)} %gate_any.1), custom_call_target="tpu_custom_call" | custom-call | tf_op jit(solution)/shard_map/pallas_call | solution.py:243
  143.4 1.1 copy.8

commit v6 on v5

--- a/solution.py
+++ b/solution.py
@@ -71,6 +71,9 @@
 
     barrier = pltpu.get_barrier_semaphore()
 
+    for r, b in reversed(PEERS):
+        pl.semaphore_signal(barrier, inc=1, device_id=device(peer(r, b)), device_id_type=MESH)
+
     @pl.when(leaves_ahead)
     def _():
         pl.semaphore_signal(barrier, inc=1, device_id=onward, device_id_type=MESH)
@@ -79,8 +82,6 @@
     def _():
         pl.semaphore_signal(barrier, inc=1, device_id=backward, device_id_type=MESH)
 
-    for r, b in PEERS:
-        pl.semaphore_signal(barrier, inc=1, device_id=device(peer(r, b)), device_id_type=MESH)
     mine = heads_at((zlo, seq))
     small = [
         pltpu.make_async_copy(noise_any, noise_ref, small_sem.at[0]),

time: 145 us -> 145 us (level)
  no operation moved by 1% of the time
where the time goes in v6:
time: 145 us
  Pallas kernels  143 us (99%)
    pallas_call x1, Pallas kernels, shards(): pl.pallas_call(functools.partial(kernel, rings), out_shape=pltpu.VMEM(que...  143 us

profile of v6, /device:TPU:1, one launch (start us, length us, event | category | flops | bytes accessed | tf_op | source)
XLA Modules:
  0.0 144.6 jit_solution(4165443305439131691)
XLA Ops:
  0.0 143.4 %shard_map.64 = bf16[128,6144]{1,0:T(8,128)(2,1)S(1)} custom-call(bf16[128,6144]{1,0:T(8,128)(2,1)} %q_ref.1, bf16[128,6144]{1,0:T(8,128)(2,1)} %k_ref.1, bf16[128,6144]{1,0:T(8,128)(2,1)} %v_ref.1, s32[64]{0:T(128)} %noise_any.1, s32[3,64]{1,0:T(4,128)} %bitcast.1, f32[8,6144]{1,0:T(8,128)} %gate_any.1), custom_call_target="tpu_custom_call" | custom-call | tf_op jit(solution)/shard_map/pallas_call | solution.py:244
  143.4 1.1 copy.8
